TPU v7x, 1024 devices: a whole 8x8x8 slice. The times are simulated.
1024 devices in a mesh: ctx: 128 (over z, y, core), head: 8 (over x).
Axes of the slice: x: 8, y: 8, z: 8, core: 2. Of those that a mesh axis runs over, the one named last changes fastest.
Arguments:
- keys: bfloat16 [8, 32768, 512], P('head', 'ctx'), may hold values from -24 to 24
- values: bfloat16 [8, 32768, 512], P('head', 'ctx'), may hold values from -6 to 6
- queries: bfloat16 [8, 32768, 512], P('head', 'ctx'), may hold values from -6 to 6
- token_lr: float32 [8, 32768], P('head', 'ctx'), may hold values from 0.005 to 0.05
- w_gate: bfloat16 [8, 512, 512], P('head'), may hold values from -0.25 to 0.25
- w_up: bfloat16 [8, 512, 512], P('head'), may hold values from -0.25 to 0.25
- w_down: bfloat16 [8, 512, 512], P('head'), may hold values from -0.25 to 0.25
- mom_gate: float32 [8, 512, 512], P('head', 'ctx'), may hold values from -6 to 6
- mom_up: float32 [8, 512, 512], P('head', 'ctx'), may hold values from -6 to 6
Outputs:
- applied: bfloat16 [8, 32768, 512], P('head', 'ctx')
- new_mom_gate: float32 [8, 512, 512], P('head', 'ctx')
- new_mom_up: float32 [8, 512, 512], P('head', 'ctx')
All inputs are finite; a program needn't handle non-finite values.
Results may differ from a plain program's by a relative error of at most 0.008.
Values may be sent and summed in bfloat16 or wider, within the bound.
A program may use at most 32 MiB of HBM per device.

v0:
```python
import jax
import jax.numpy as jnp
from jax import lax
from jax.sharding import PartitionSpec as P


def key_product(keys, factor):
    return lax.dot_general(
        keys, factor, (((0,), (0,)), ((), ())), preferred_element_type=jnp.float32
    )


def row_step(moment, grads, weight_rows):
    fresh = 0.9 * moment + grads
    step = fresh / jnp.sqrt(jnp.mean(fresh * fresh, axis=-1, keepdims=True) + 1e-05)
    return (fresh, (weight_rows.astype(jnp.float32) - 0.02 * step).astype(jnp.bfloat16))


def per_device(keys, values, queries, token_lr, w_gate, w_up, w_down, mom_gate, mom_up):
    key_rows = keys[0]
    query_rows = queries[0]
    gate_full = w_gate[0]
    up_full = w_up[0]
    down_full = w_down[0]
    pre_gate = jnp.dot(key_rows, gate_full, preferred_element_type=jnp.float32)
    pre_up = jnp.dot(key_rows, up_full, preferred_element_type=jnp.float32)
    dout = (-token_lr[0][:, None] * values[0].astype(jnp.float32)).astype(jnp.bfloat16)
    zgrad = lax.dot_general(
        dout, down_full, (((1,), (1,)), ((), ())), preferred_element_type=jnp.float32
    )
    sig = jax.nn.sigmoid(pre_gate)
    grad_gate = (zgrad * pre_up * sig * (1.0 + pre_gate * (1.0 - sig))).astype(jnp.bfloat16)
    grad_up = (zgrad * pre_gate * sig).astype(jnp.bfloat16)
    owned = mom_gate.shape[1]
    g_gate = lax.psum_scatter(
        key_product(key_rows, grad_gate), "ctx", scatter_dimension=0, tiled=True
    )
    g_up = lax.psum_scatter(key_product(key_rows, grad_up), "ctx", scatter_dimension=0, tiled=True)
    first_row = lax.axis_index("ctx") * owned
    gate_rows = lax.dynamic_slice_in_dim(gate_full, first_row, owned, 0)
    up_rows = lax.dynamic_slice_in_dim(up_full, first_row, owned, 0)
    fresh_gate, next_gate = row_step(mom_gate[0], g_gate, gate_rows)
    fresh_up, next_up = row_step(mom_up[0], g_up, up_rows)
    q_gate = jnp.dot(
        query_rows,
        lax.all_gather(next_gate, "ctx", axis=0, tiled=True),
        preferred_element_type=jnp.float32,
    )
    q_up = jnp.dot(
        query_rows,
        lax.all_gather(next_up, "ctx", axis=0, tiled=True),
        preferred_element_type=jnp.float32,
    )
    hidden = (jax.nn.silu(q_gate) * q_up).astype(jnp.bfloat16)
    applied = jnp.dot(hidden, down_full, preferred_element_type=jnp.float32).astype(jnp.bfloat16)
    return (applied[None], fresh_gate[None], fresh_up[None])


def solution(mesh):
    return jax.shard_map(
        per_device,
        mesh=mesh,
        in_specs=(
            P("head", "ctx", None),
            P("head", "ctx", None),
            P("head", "ctx", None),
            P("head", "ctx"),
            P("head", None, None),
            P("head", None, None),
            P("head", None, None),
            P("head", "ctx", None),
            P("head", "ctx", None),
        ),
        out_specs=(P("head", "ctx", None), P("head", "ctx", None), P("head", "ctx", None)),
        check_vma=False,
    )
```

profile of v0, /device:TPU:1, one launch (start us, length us, event | category | flops | bytes accessed | tf_op | source)
XLA Modules:
  0.0 350.9 jit_solution(16024431288592967702)
XLA Ops:
  7.2 0.0 copy-start
  7.2 0.0 all-reduce.5.cloned.1.call-start
  7.2 0.7 neg.18
  8.0 0.0 copy-start.3
  8.0 1.5 fusion.6
  9.4 0.0 copy-done
  9.4 0.0 copy-done.3
  9.4 0.0 copy-start.1
  9.5 0.3 fusion.11
  9.8 0.6 copy-done.1
  10.4 0.0 copy-start.6
  10.4 1.4 convolution_bitcast_fusion
  11.8 0.0 copy-done.6
  11.8 1.6 convolution_bitcast_fusion.1
  13.4 0.0 all-reduce.5.cloned.1.call-update
  13.4 0.0 copy-start.4
  13.4 0.7 copy-done.4
  14.1 0.0 copy-start.5
  14.1 0.1 copy.29
  14.3 0.5 copy-done.5
  14.8 0.1 copy.33
  15.0 0.7 constant_dynamic-slice_fusion
  15.7 0.2 copy.44
  15.9 0.2 copy.45
  16.1 1.3 dynamic-slice.2
  18.0 221.3 %all-reduce.5.cloned.1.call-done = (f32[512,512]{0,1:T(8,128)}, f32[512,512]{0,1:T(8,128)}) async-done(((f32[512,512]{0,1:T(8,128)}, f32[512,512]{0,1:T(8,128)}), (f32[512,512]{0,1:T(8,128)}, f32[512,512]{0,1:T(8,128)})) %all-reduce.5.cloned.1.call-update) | async-done | bytes 2097168
  239.3 1.2 multiply_reduce_fusion
  240.5 0.1 fusion.36
  240.6 0.1 copy.30
  240.7 52.6 %all-gather = bf16[128,4,512]{2,1,0:T(4,128)(2,1)S(1)} all-gather(bf16[1,4,512]{2,1,0:T(4,128)(2,1)S(1)} %copy.30), channel_id=1, replica_groups=mesh['ctx'=128,'head'=8] {'ctx'}, dimensions={0}, use_global_device_ids=true | all-gather | bytes 528384 | tf_op jit(solution)/shard_map/all_gather | solution.py:46
  293.3 0.1 reshape.51
  293.5 0.1 copy.34
  293.6 47.3 %all-gather.1 = bf16[128,4,512]{2,1,0:T(4,128)(2,1)S(1)} all-gather(bf16[1,4,512]{2,1,0:T(4,128)(2,1)S(1)} %copy.34), channel_id=1, replica_groups=mesh['ctx'=128,'head'=8] {'ctx'}, dimensions={0}, use_global_device_ids=true | all-gather | bytes 528384 | tf_op jit(solution)/shard_map/all_gather | solution.py:51
  341.0 0.1 reshape.53
  341.1 0.0 copy-start.2
  341.1 0.7 copy.36
  341.8 0.7 copy.37
  342.5 0.0 copy-done.2
  342.5 0.3 convolution_bitcast_fusion.3
  342.8 1.2 fusion.5
  (3 shorter events, 0.1 us)
Async XLA Ops:
  7.2 2.3 copy-start
  7.2 232.1 %all-reduce.5.cloned.1.call-start = ((), (), s32[]{:S(2)}) async-start(), calls=%async_computation | async-start | bytes 4194304
  8.0 1.5 copy-start.3
  9.4 1.0 copy-start.1
  10.4 1.4 copy-start.6
  13.4 0.7 copy-start.4
  14.1 0.7 copy-start.5
  341.1 1.4 copy-start.2
Sparse Core Ops, SparseCore 0:
  13.5 225.6 all-reduce.4
where the time goes:
time: 351 us
  waiting for transfers between devices  221 us (63%)
  blocking collectives  100 us (28%)
  between operations  14.8 us (4%)
  local copies, waits for them, and re-layouts  6.35 us (2%)
  matrix products  6.31 us (2%)
    unnamed x2, waiting for transfers between devices  221 us
    all_gather x1, blocking collectives, per_device(): lax.all_gather(next_gate, 'ctx', axis=0, tiled=True)  52.6 us
    all_gather x1, blocking collectives, per_device(): lax.all_gather(next_up, 'ctx', axis=0, tiled=True)  47.3 us
  transfers between devices with their start and end apart: 1, of which 1 were waited for; matrix products, arithmetic and copies ran while one was open for 1% of the time, Pallas kernels for 0%

commit v1 on v0

v1 whole, which is shorter than its diff:
```python
import jax
import jax.numpy as jnp
from jax import lax
from jax.experimental import pallas as pl
from jax.experimental.pallas import tpu as pltpu
from jax.sharding import PartitionSpec as P

MESH = pl.DeviceIdType.MESH
F32, BF16 = jnp.float32, jnp.bfloat16
RING = 8
D = 512
T = 256
OFFSETS = (0, 1, -1, 2, -2, 3, -3, 4)


def dot(a, b):
    return jnp.dot(a, b, preferred_element_type=F32)


def dot_t(a, b):
    return lax.dot_general(a, b, (((1,), (1,)), ((), ())), preferred_element_type=F32)


def ring(v):
    return lax.rem(v + RING, RING)


def selector(z, y, matrix, sign, wide):
    rows = D * 2 if wide else D
    row = lax.broadcasted_iota(jnp.int32, (rows, 128), 0)
    lane = lax.broadcasted_iota(jnp.int32, (rows, 128), 1)
    low = 4 if wide else 3
    first, second = row >> (low + 3), (row >> low) & 7

    def place(origin, slot):
        off = jnp.where((slot & 1) == 1, (slot + 1) >> 1, -(slot >> 1))
        return (origin + sign * off + RING) & (RING - 1)

    if matrix == 0:
        chip = place(z, second) * RING + place(y, first)
    else:
        chip = place(z, first) * RING + place(y, second)
    feature = chip * 8 + (row & 7)
    if wide:
        feature = jnp.where((row & 8) == 0, feature, -1)
    parts = [
        jnp.where(feature == lane + 128 * k, 1.0, 0.0).astype(BF16) for k in range(D // 128)
    ]
    return jnp.concatenate(parts, axis=1)


def stack(block):
    return jnp.concatenate([block[:, : D // 2], block[:, D // 2 :]], axis=0)


def kernel(
    keys, values, queries, lr, w_gate, w_up, w_down, mom_gate, mom_up,
    out, out_gate, out_up,
    keys_v, values_v, queries_v, lr_v, w_v, down_v, mom_v, mom_in, mom_send, mom_recv,
    keys_t, grads, pair_send, pair_recv, hop_send, hop_recv, total, rows_send, rows_recv,
    weights, q_left, q_right,
    load_sem, pair_ss, pair_rs, hop_ss, hop_rs, row_ss, row_rs,
    near_ss, near_rs, far_ss, far_rs, fwd_ss, fwd_rs, mom_ss, mom_rs,
):
    me = lax.axis_index("ctx")
    c = lax.rem(me, 2)
    chip = lax.div(me, 2)
    y = lax.rem(chip, RING)
    z = lax.div(chip, RING)
    mine, other = c, 1 - c

    def device(zz, yy, cc):
        return {"ctx": (ring(zz) * RING + ring(yy)) * 2 + cc}

    partner = device(z, y, 1 - c)
    first = [device(z + c * o, y + (1 - c) * o, c) for o in OFFSETS]
    second = [device(z + (1 - c) * o, y + c * o, c) for o in OFFSETS]

    loads = [
        pltpu.make_async_copy(src, dst, load_sem.at[k])
        for k, (src, dst) in enumerate(
            (
                (keys.at[0], keys_v),
                (w_gate.at[0], w_v.at[0]),
                (w_up.at[0], w_v.at[1]),
                (lr, lr_v),
                (values.at[0], values_v),
                (w_down.at[0], down_v),
                (mom_gate.at[0], mom_v.at[0]),
                (mom_up.at[0], mom_v.at[1]),
                (queries.at[0], queries_v),
            )
        )
    ]
    for load in loads:
        load.start()

    barrier = pltpu.get_barrier_semaphore()
    for peer in [partner] + first[1:] + second[1:]:
        pl.semaphore_signal(barrier, inc=1, device_id=peer, device_id_type=MESH)

    def remote(src, dst, ss, rs, to):
        return pltpu.make_async_remote_copy(
            src_ref=src, dst_ref=dst, send_sem=ss, recv_sem=rs, device_id=to, device_id_type=MESH
        )

    pick = [selector(z, y, m, 1, False) for m in range(2)]
    loads[0].wait()
    for m in range(2):
        keys_t[m] = dot_t(pick[m], keys_v[...]).astype(BF16)
    for k in (1, 2, 3, 4, 5):
        loads[k].wait()
    rate = jnp.broadcast_to(lr_v[...], (128, T)).T
    rate = jnp.concatenate([rate] * (D // 128), axis=1)
    dout = (-rate * values_v[...].astype(F32)).astype(BF16)
    for h in range(2):
        cols = pl.ds(h * (D // 2), D // 2)
        gate = dot(keys_v[...], w_v[0, :, cols])
        up = dot(keys_v[...], w_v[1, :, cols])
        zgrad = dot_t(dout, down_v[cols, :])
        sig = jax.nn.sigmoid(gate)
        zs = zgrad * sig
        grads[0, :, cols] = (zs * up * (1.0 + gate * (1.0 - sig))).astype(BF16)
        grads[1, :, cols] = (zs * gate).astype(BF16)

    pl.semaphore_wait(barrier, 2 * RING - 1)

    groups = (3, 2, 1, 0)
    pairs = []
    for g in groups:
        rows = pl.ds(g * 128, 128)
        pair_send[rows, :] = dot(keys_t[other, rows, :], grads[other]).astype(BF16)
        copy = remote(pair_send.at[rows], pair_recv.at[rows], pair_ss.at[g], pair_rs.at[g], partner)
        copy.start()
        pairs.append(copy)
    loads[6].wait()
    loads[7].wait()
    mom_copy = remote(mom_v.at[other], mom_in, mom_ss.at[0], mom_rs.at[0], partner)
    mom_copy.start()

    hops = [None] * RING
    for copy, g in zip(pairs, groups):
        rows = pl.ds(g * 128, 128)
        part = dot(keys_t[mine, rows, :], grads[mine])
        copy.wait_recv()
        part = part + pair_recv[rows, :].astype(F32)
        for j in (2 * g + 1, 2 * g):
            half = part[64:] if j % 2 else part[:64]
            if j == 0:
                total[...] = half
            else:
                hop_send[j] = half.astype(BF16)
                hops[j] = remote(
                    hop_send.at[j], hop_recv.at[j], hop_ss.at[j], hop_rs.at[j], first[j]
                )
                hops[j].start()

    loads[8].wait()
    for m in range(2):
        left = dot_t(queries_v[...], selector(z, y, m, -1, True))
        q_left[m] = left.astype(BF16)
        q_right[m] = pltpu.roll(left, 8, 1).astype(BF16)
    pair_row = pl.multiple_of(lax.div(chip, 2) * 16, 16)
    w_rows = w_v[mine, pl.ds(pair_row, 16), :].astype(F32)
    w_rows = stack(jnp.where(lax.rem(chip, 2) == 0, w_rows[:8], w_rows[8:]))
    mom_copy.wait_recv()
    own, theirs = mom_v[mine], mom_in[...]
    even = c == 0
    momentum = stack(
        jnp.concatenate([jnp.where(even, own, theirs), jnp.where(even, theirs, own)], axis=0)
    )

    acc = total[...]
    for j in range(1, RING):
        hops[j].wait_recv()
        acc = acc + hop_recv[j].astype(F32)

    row_copies = [None] * RING
    for d in range(RING - 1, 0, -1):
        rows_send[d] = stack(acc[d * 8 : d * 8 + 8]).astype(BF16)
        row_copies[d] = remote(
            rows_send.at[d], rows_recv.at[d], row_ss.at[d], row_rs.at[d], second[d]
        )
        row_copies[d].start()
    grad = stack(acc[:8])
    for d in range(1, RING):
        row_copies[d].wait_recv()
        grad = grad + rows_recv[d].astype(F32)
    fresh = 0.9 * momentum + grad
    square = jnp.sum(fresh * fresh, axis=1, keepdims=True)
    square = (square[:8] + square[8:]) * (1.0 / D)
    scale = 1.0 / jnp.sqrt(jnp.concatenate([square, square], axis=0) + 1e-05)
    weights[mine, pl.ds(0, 16), :] = (w_rows - 0.02 * (fresh * scale)).astype(BF16)

    near = [None] * RING
    for d in range(RING - 1, 0, -1):
        near[d] = remote(
            weights.at[mine, pl.ds(0, 16)],
            weights.at[mine, pl.ds(16 * d, 16)],
            near_ss.at[d], near_rs.at[d], second[d],
        )
        near[d].start()
    whole = jnp.concatenate([fresh[:8], fresh[8:]], axis=1)
    keep = jnp.where(even, whole[:4], whole[4:])
    mom_send[...] = jnp.where(even, whole[4:], whole[:4])
    mom_back = remote(mom_send, mom_recv, mom_ss.at[1], mom_rs.at[1], partner)
    mom_back.start()
    for d in range(1, RING):
        near[d].wait_recv()

    far = [None] * RING
    block = lambda j: weights.at[mine, pl.ds(128 * j, 128)]
    for j in range(RING - 1, 0, -1):
        far[j] = remote(block(0), block(j), far_ss.at[j], far_rs.at[j], first[j])
        far[j].start()
    forward = []
    for j in range(RING):
        if j:
            far[j].wait_recv()
        copy = remote(block(j), block(j), fwd_ss.at[j], fwd_rs.at[j], partner)
        copy.start()
        forward.append(copy)
    mom_back.wait_recv()
    back = mom_recv[...]
    out_gate[0] = jnp.where(even, keep, back)
    out_up[0] = jnp.where(even, back, keep)
    for copy in forward:
        copy.wait_recv()

    for h in range(2):
        cols = pl.ds(h * (D // 2), D // 2)
        q = q_left if h == 0 else q_right
        gate = dot(q[0], weights[0])
        up = dot(q[1], weights[1])
        grads[0, :, cols] = (gate * jax.nn.sigmoid(gate) * up).astype(BF16)
    out[0] = dot(grads[0], down_v[...]).astype(BF16)

    for copy in pairs + hops[1:] + row_copies[1:] + near[1:] + far[1:] + forward + [mom_copy, mom_back]:
        copy.wait_send()


def per_device(*args):
    hbm = pl.BlockSpec(memory_space=pltpu.HBM)
    vmem = pl.BlockSpec(memory_space=pltpu.VMEM)
    dma = pltpu.SemaphoreType.DMA
    return pl.pallas_call(
        kernel,
        out_shape=(
            jax.ShapeDtypeStruct((1, T, D), BF16),
            jax.ShapeDtypeStruct((1, 4, D), F32),
            jax.ShapeDtypeStruct((1, 4, D), F32),
        ),
        in_specs=[hbm] * 9,
        out_specs=(vmem, vmem, vmem),
        scratch_shapes=[
            pltpu.VMEM((T, D), BF16),
            pltpu.VMEM((T, D), BF16),
            pltpu.VMEM((T, D), BF16),
            pltpu.VMEM((1, T), F32),
            pltpu.VMEM((2, D, D), BF16),
            pltpu.VMEM((D, D), BF16),
            pltpu.VMEM((2, 4, D), F32),
            pltpu.VMEM((4, D), F32),
            pltpu.VMEM((4, D), F32),
            pltpu.VMEM((4, D), F32),
            pltpu.VMEM((2, D, T), BF16),
            pltpu.VMEM((2, T, D), BF16),
            pltpu.VMEM((D, D), BF16),
            pltpu.VMEM((D, D), BF16),
            pltpu.VMEM((RING, 64, D), BF16),
            pltpu.VMEM((RING, 64, D), BF16),
            pltpu.VMEM((64, D), F32),
            pltpu.VMEM((RING, 16, D // 2), BF16),
            pltpu.VMEM((RING, 16, D // 2), BF16),
            pltpu.VMEM((2, 2 * D, D // 2), BF16),
            pltpu.VMEM((2, T, 2 * D), BF16),
            pltpu.VMEM((2, T, 2 * D), BF16),
            dma((9,)),
            dma((4,)), dma((4,)),
            dma((RING,)), dma((RING,)),
            dma((RING,)), dma((RING,)),
            dma((RING,)), dma((RING,)),
            dma((RING,)), dma((RING,)),
            dma((RING,)), dma((RING,)),
            dma((2,)), dma((2,)),
        ],
        compiler_params=pltpu.CompilerParams(
            collective_id=0, has_side_effects=True, vmem_limit_bytes=63_000_000
        ),
        cost_estimate=pl.CostEstimate(
            flops=16 * T * D * D, bytes_accessed=3 * 1024 * 1024, transcendentals=2 * T * D
        ),
        name="update_and_apply",
    )(*args)


def solution(mesh):
    tokens = P("head", "ctx", None)
    weight = P("head", None, None)
    return jax.shard_map(
        per_device,
        mesh=mesh,
        in_specs=(tokens, tokens, tokens, P("head", "ctx"), weight, weight, weight, tokens, tokens),
        out_specs=(tokens, tokens, tokens),
        check_vma=False,
    )
```

time: 351 us -> 57.6 us (0.16)
  waiting for transfers between devices: 221 us -> 0 us
  blocking collectives: 100 us -> 0 us
  Pallas kernels: 0 us -> 53.6 us
  between operations: 14.8 us -> 0.65 us
  matrix products: 6.31 us -> 0 us
    unnamed x2 -> x0, waiting for transfers between devices: 221 us -> none
    all_gather x2 -> x0, blocking collectives: 100 us -> none  [the longest x1 52.6 us: per_device(): lax.all_gather(next_gate, 'ctx', axis=0, tiled=True)]
    pallas_call x0 -> x1, Pallas kernels: none -> 53.6 us  [per_device(): pl.pallas_call(kernel, out_shape=(jax.ShapeDtypeStruct((1, T, D), BF16),...]
    dot_general x6 -> x0, matrix products: 6.31 us -> none  [the longest x2 3 us: key_product(): lax.dot_general(keys, factor, (((0,), (0,)), ((), ())), preferred_element...]
  transfers between devices with their start and end apart: 1 -> 0, of which waited for: 1 -> 0; matrix products, arithmetic and copies ran while one was open for 1% -> 0% of each run, Pallas kernels for 0% -> 0%
where the time goes in v1:
time: 57.6 us; the launch traced here: 57.2 us
  Pallas kernels  53.6 us (93%)
  local copies, waits for them, and re-layouts  2.98 us (5%)
  between operations  0.65 us (1%)
    pallas_call x1, Pallas kernels, per_device(): pl.pallas_call(kernel, out_shape=(jax.ShapeDtypeStruct((1, T, D), BF16),...  53.6 us
    unnamed x7, local copies, waits for them, and re-layouts  2.98 us

profile of v1, /device:TPU:1, one launch (start us, length us, event | category | flops | bytes accessed | tf_op | source)
XLA Modules:
  0.0 57.2 jit_solution(7394472468908208828)
XLA Ops:
  0.6 53.6 %update_and_apply.1 = (bf16[1,256,512]{2,1,0:T(8,128)(2,1)}, f32[1,4,512]{2,1,0:T(4,128)}, f32[1,4,512]{2,1,0:T(4,128)}) custom-call(bf16[1,256,512]{2,1,0:T(8,128)(2,1)} %keys.1, bf16[1,256,512]{2,1,0:T(8,128)(2,1)} %values.1, bf16[1,256,512]{2,1,0:T(8,128)(2,1)} %queries.1, f32[1,256]{1,0:T(1,128)} %lr.1, bf16[1,512,512]{2,1,0:T(8,128)(2,1)} %w_gate.1, ...), custom_call_target="tpu_custom_call" | custom-call | flops 1073741824 | bytes 3145728 | tf_op jit(solution)/shard_map/update_and_apply/pallas_call | solution.py:246
  54.2 0.0 copy-start.1
  54.2 1.7 %copy.15 = bf16[1,256,512]{2,1,0:T(8,128)(2,1)} copy(bf16[1,256,512]{2,1,0:T(8,128)(2,1)} %get-tuple-element.6) | data formatting | bytes 524288
  55.9 0.0 copy-done.1
  55.9 0.0 copy-start
  55.9 0.6 %copy.16 = f32[1,4,512]{2,1,0:T(4,128)} copy(f32[1,4,512]{2,1,0:T(4,128)S(1)} %copy-done.1) | data formatting | bytes 16384
  56.5 0.1 copy-done
  56.6 0.6 %copy.17 = f32[1,4,512]{2,1,0:T(4,128)} copy(f32[1,4,512]{2,1,0:T(4,128)S(1)} %copy-done) | data formatting | bytes 16384
Async XLA Ops:
  54.2 1.7 %copy-start.1 = (f32[1,4,512]{2,1,0:T(4,128)S(1)}, f32[1,4,512]{2,1,0:T(4,128)}, u32[]{:S(2)}) copy-start(f32[1,4,512]{2,1,0:T(4,128)} %get-tuple-element.7) | copy-start | bytes 24580
  55.9 0.7 %copy-start = (f32[1,4,512]{2,1,0:T(4,128)S(1)}, f32[1,4,512]{2,1,0:T(4,128)}, u32[]{:S(2)}) copy-start(f32[1,4,512]{2,1,0:T(4,128)} %get-tuple-element.8) | copy-start | bytes 24580

commit v2 on v1

v2 whole, which is shorter than its diff:
```python
import jax
import jax.numpy as jnp
from jax import lax
from jax.experimental import pallas as pl
from jax.experimental.pallas import tpu as pltpu
from jax.sharding import PartitionSpec as P

MESH = pl.DeviceIdType.MESH
F32, BF16 = jnp.float32, jnp.bfloat16
RING = 8
D = 512
T = 256
Y_ORDER = (1, 0, 2, 3, 7, 6, 4, 5)
Z_ORDER = (0, 1, 2, 3, 4, 5, 6, 7)
NEAR_FIRST = (1, 7, 2, 6, 3, 5, 4)


def dot(a, b):
    return jnp.dot(a, b, preferred_element_type=F32)


def dot_t(a, b):
    return lax.dot_general(a, b, (((1,), (1,)), ((), ())), preferred_element_type=F32)


def one_hot(picked, width):
    lane = lax.broadcasted_iota(jnp.int32, picked.shape, 1)
    parts = [
        jnp.where(picked == lane + 128 * k, 1.0, 0.0).astype(BF16) for k in range(width // 128)
    ]
    return jnp.concatenate(parts, axis=1)


def swapped(row):
    return ((row >> 3) & 7) * 64 + (row >> 6) * 8 + (row & 7)


def kernel(
    keys, values, queries, lr, w_gate, w_up, w_down, mom_gate, mom_up,
    out, out_gate, out_up,
    keys_v, values_v, queries_v, lr_v, w_v, down_v, mom_v, mom_in, mom_send, mom_recv,
    keys_t, grads, pair_send, pair_recv, hop_send, hop_recv, total, part_send, part_recv,
    weights, queries_p,
    load_sem, pair_ss, pair_rs, hop_ss, hop_rs, part_ss, part_rs,
    far_ss, far_rs, fwd_ss, fwd_rs, mom_ss, mom_rs,
):
    me = lax.axis_index("ctx")
    c = lax.rem(me, 2)
    chip = lax.div(me, 2)
    y = lax.rem(chip, RING)
    z = lax.div(chip, RING)
    mine, other = c, 1 - c
    even = c == 0
    at1 = jnp.where(even, y, z)
    at2 = jnp.where(even, z, y)
    partner = {"ctx": me + 1 - 2 * c}

    def first(s):
        return {"ctx": jnp.where(even, z * RING + s, s * RING + y) * 2 + c}

    def second(s):
        return {"ctx": jnp.where(even, s * RING + y, z * RING + s) * 2 + c}

    def beside(at, k):
        return (at + k) & (RING - 1)

    loads = [
        pltpu.make_async_copy(src, dst, load_sem.at[k])
        for k, (src, dst) in enumerate(
            (
                (keys.at[0], keys_v),
                (w_gate.at[0], w_v.at[0]),
                (w_up.at[0], w_v.at[1]),
                (lr, lr_v),
                (values.at[0], values_v),
                (w_down.at[0], down_v),
                (mom_gate.at[0], mom_v.at[0]),
                (mom_up.at[0], mom_v.at[1]),
                (queries.at[0], queries_v),
            )
        )
    ]
    for load in loads:
        load.start()

    barrier = pltpu.get_barrier_semaphore()
    for peer in (
        [partner]
        + [first(beside(at1, k)) for k in range(1, RING)]
        + [second(beside(at2, k)) for k in range(1, RING)]
    ):
        pl.semaphore_signal(barrier, inc=1, device_id=peer, device_id_type=MESH)

    def remote(src, dst, ss, rs, to):
        return pltpu.make_async_remote_copy(
            src_ref=src, dst_ref=dst, send_sem=ss, recv_sem=rs, device_id=to, device_id_type=MESH
        )

    eye = one_hot(lax.broadcasted_iota(jnp.int32, (D, 128), 0), D)
    loads[0].wait()
    turned = dot_t(eye, keys_v[...])
    keys_t[1] = turned.astype(BF16)
    keys_t[0] = jnp.concatenate(
        [turned[64 * b + 8 * a : 64 * b + 8 * a + 8] for a in range(RING) for b in range(RING)], axis=0
    ).astype(BF16)
    for k in (1, 2, 3, 4, 5):
        loads[k].wait()
    rate = jnp.broadcast_to(lr_v[...], (128, T)).T
    rate = jnp.concatenate([rate] * (D // 128), axis=1)
    dout = (-rate * values_v[...].astype(F32)).astype(BF16)
    for h in range(2):
        cols = pl.ds(h * (D // 2), D // 2)
        gate = dot(keys_v[...], w_v[0, :, cols])
        up = dot(keys_v[...], w_v[1, :, cols])
        zgrad = dot_t(dout, down_v[cols, :])
        sig = jax.nn.sigmoid(gate)
        zs = zgrad * sig
        grads[0, :, cols] = (zs * up * (1.0 + gate * (1.0 - sig))).astype(BF16)
        grads[1, :, cols] = (zs * gate).astype(BF16)

    pl.semaphore_wait(barrier, 2 * RING - 1)

    turns = (2, 1, 3, 0)
    theirs = jnp.where(even, z, y) >> 1
    pairs = []
    for t in turns:
        g = (theirs + t) & 3
        rows = pl.ds(pl.multiple_of(g * 128, 128), 128)
        pair_send[rows, :] = dot(keys_t[other, rows, :], grads[other]).astype(BF16)
        copy = remote(pair_send.at[rows], pair_recv.at[rows], pair_ss.at[t], pair_rs.at[t], partner)
        copy.start()
        pairs.append(copy)
    loads[6].wait()
    loads[7].wait()
    mom_copy = remote(mom_v.at[other], mom_in, mom_ss.at[0], mom_rs.at[0], partner)
    mom_copy.start()

    def hop(s):
        return remote(hop_send.at[s], hop_recv.at[at1], hop_ss.at[s], hop_rs.at[at1], first(s))

    for copy, t in zip(pairs, turns):
        g = ((at1 >> 1) + t) & 3
        rows = pl.ds(pl.multiple_of(g * 128, 128), 128)
        part = dot(keys_t[mine, rows, :], grads[mine])
        copy.wait_recv()
        part = part + pair_recv[rows, :].astype(F32)
        if t:
            for half in range(2):
                s = 2 * g + half
                hop_send[s] = part[64 * half : 64 * half + 64].astype(BF16)
                hop(s).start()
        else:
            low = (at1 & 1) == 0
            total[...] = jnp.where(low, part[:64], part[64:])
            s = at1 + 1 - 2 * (at1 & 1)
            hop_send[s] = jnp.where(low, part[64:], part[:64]).astype(BF16)
            hop(s).start()

    loads[8].wait()
    order = one_hot(swapped(lax.broadcasted_iota(jnp.int32, (D, 128), 0)), D)
    queries_p[...] = dot_t(queries_v[...], order).astype(BF16)
    row = lax.broadcasted_iota(jnp.int32, (64, 128), 0)
    feature = jnp.where(even, (row >> 3) * 64 + at1 * 8 + (row & 7), at1 * 64 + row)
    w_rows = dot(one_hot(feature, D), w_v[mine])
    mom_copy.wait_recv()
    own, given = mom_v[mine], mom_in[...]
    here = pl.ds(pl.multiple_of(at2 * 8, 8), 8)
    momentum = jnp.concatenate([jnp.where(even, own, given), jnp.where(even, given, own)], axis=0)
    total[here, :] = total[here, :] + 0.9 * momentum

    acc = total[...]
    for k in NEAR_FIRST:
        s = beside(at1, k)
        remote(hop_send.at[s], hop_recv.at[s], hop_ss.at[s], hop_rs.at[s], first(s)).wait_recv()
        acc = acc + hop_recv[s].astype(F32)
    part_send[...] = acc.astype(BF16)

    def share(s):
        return remote(part_send, part_recv.at[at2], part_ss.at[s], part_rs.at[at2], second(s))

    for sy, sz in zip(Y_ORDER, Z_ORDER):
        s = jnp.where(even, sz, sy)

        @pl.when(s != at2)
        def _(s=s):
            share(s).start()

    for k in NEAR_FIRST:
        s = beside(at2, k)
        remote(part_send, part_recv.at[s], part_ss.at[s], part_rs.at[s], second(s)).wait_recv()
        acc = acc + part_recv[s].astype(F32)
    scale = 0.02 / jnp.sqrt(jnp.mean(acc * acc, axis=1, keepdims=True) + 1e-05)

    def block(s):
        return weights.at[mine, pl.ds(pl.multiple_of(s * 64, 64), 64)]

    block(at1)[...] = (w_rows - acc * scale).astype(BF16)

    def spread(s):
        return remote(block(at1), block(at1), far_ss.at[s], far_rs.at[at1], first(s))

    def forward(s):
        return remote(block(s), block(s), fwd_ss.at[s], fwd_rs.at[s], partner)

    for sy, sz in zip(Y_ORDER, Z_ORDER):
        s = jnp.where(even, sy, sz)

        @pl.when(s != at1)
        def _(s=s):
            spread(s).start()

    forward(at1).start()
    total[...] = acc
    fresh = total[here, :]
    keep = jnp.where(even, fresh[:4], fresh[4:])
    mom_send[...] = jnp.where(even, fresh[4:], fresh[:4])
    mom_back = remote(mom_send, mom_recv, mom_ss.at[1], mom_rs.at[1], partner)
    mom_back.start()
    for k in NEAR_FIRST:
        s = beside(at1, k)
        remote(block(s), block(s), far_ss.at[s], far_rs.at[s], first(s)).wait_recv()
        forward(s).start()
    mom_back.wait_recv()
    back = mom_recv[...]
    out_gate[0] = jnp.where(even, keep, back)
    out_up[0] = jnp.where(even, back, keep)
    for s in range(RING):
        theirs_s = weights.at[other, pl.ds(64 * s, 64)]
        remote(theirs_s, theirs_s, fwd_ss.at[s], fwd_rs.at[s], partner).wait_recv()

    for h in range(2):
        cols = pl.ds(h * (D // 2), D // 2)
        gate = dot(queries_p[...], weights[0, :, cols])
        up = dot(queries_v[...], weights[1, :, cols])
        grads[0, :, cols] = (gate * jax.nn.sigmoid(gate) * up).astype(BF16)
    out[0] = dot(grads[0], down_v[...]).astype(BF16)

    for k in range(1, RING):
        hop(beside(at1, k)).wait_send()
        share(beside(at2, k)).wait_send()
        spread(beside(at1, k)).wait_send()
    for s in range(RING):
        forward(s).wait_send()
    for copy in pairs + [mom_copy, mom_back]:
        copy.wait_send()


def store_kernel(a, b, c, a_out, b_out, c_out, sem):
    copies = [
        pltpu.make_async_copy(src, dst, sem.at[k])
        for k, (src, dst) in enumerate(((a, a_out), (b, b_out), (c, c_out)))
    ]
    for copy in copies:
        copy.start()
    for copy in copies:
        copy.wait()


def per_device(*args):
    hbm = pl.BlockSpec(memory_space=pl.ANY)
    vmem = pl.BlockSpec(memory_space=pltpu.VMEM)
    dma = pltpu.SemaphoreType.DMA
    shapes = (
        jax.ShapeDtypeStruct((1, T, D), BF16),
        jax.ShapeDtypeStruct((1, 4, D), F32),
        jax.ShapeDtypeStruct((1, 4, D), F32),
    )
    results = pl.pallas_call(
        kernel,
        out_shape=tuple(pltpu.VMEM(s.shape, s.dtype) for s in shapes),
        in_specs=[hbm] * 9,
        out_specs=(vmem, vmem, vmem),
        scratch_shapes=[
            pltpu.VMEM((T, D), BF16),
            pltpu.VMEM((T, D), BF16),
            pltpu.VMEM((T, D), BF16),
            pltpu.VMEM((1, T), F32),
            pltpu.VMEM((2, D, D), BF16),
            pltpu.VMEM((D, D), BF16),
            pltpu.VMEM((2, 4, D), F32),
            pltpu.VMEM((4, D), F32),
            pltpu.VMEM((4, D), F32),
            pltpu.VMEM((4, D), F32),
            pltpu.VMEM((2, D, T), BF16),
            pltpu.VMEM((2, T, D), BF16),
            pltpu.VMEM((D, D), BF16),
            pltpu.VMEM((D, D), BF16),
            pltpu.VMEM((RING, 64, D), BF16),
            pltpu.VMEM((RING, 64, D), BF16),
            pltpu.VMEM((64, D), F32),
            pltpu.VMEM((64, D), BF16),
            pltpu.VMEM((RING, 64, D), BF16),
            pltpu.VMEM((2, D, D), BF16),
            pltpu.VMEM((T, D), BF16),
            dma((9,)),
            dma((4,)), dma((4,)),
            dma((RING,)), dma((RING,)),
            dma((RING,)), dma((RING,)),
            dma((RING,)), dma((RING,)),
            dma((RING,)), dma((RING,)),
            dma((2,)), dma((2,)),
        ],
        compiler_params=pltpu.CompilerParams(
            collective_id=0, has_side_effects=True, vmem_limit_bytes=63_000_000
        ),
        cost_estimate=pl.CostEstimate(
            flops=16 * T * D * D, bytes_accessed=3 * 1024 * 1024, transcendentals=2 * T * D
        ),
        name="update_and_apply",
    )(*args)
    return pl.pallas_call(
        store_kernel,
        out_shape=shapes,
        in_specs=[hbm] * 3,
        out_specs=(hbm, hbm, hbm),
        scratch_shapes=[dma((3,))],
        compiler_params=pltpu.CompilerParams(vmem_limit_bytes=1024 * 1024),
        name="store",
    )(*results)


def solution(mesh):
    tokens = P("head", "ctx", None)
    weight = P("head", None, None)
    return jax.shard_map(
        per_device,
        mesh=mesh,
        in_specs=(tokens, tokens, tokens, P("head", "ctx"), weight, weight, weight, tokens, tokens),
        out_specs=(tokens, tokens, tokens),
        check_vma=False,
    )
```

time: 57.6 us -> 49.7 us (0.86)
  Pallas kernels: 53.6 us -> 48.9 us
  local copies, waits for them, and re-layouts: 2.98 us -> 0 us
    pallas_call x1 -> x2, Pallas kernels: 53.6 us -> 48.9 us  [the longest x1 48.2 us: per_device(): pl.pallas_call(kernel, out_shape=tuple((pltpu.VMEM(s.shape, s.dtype) for...]
    unnamed x7 -> x0, local copies, waits for them, and re-layouts: 2.98 us -> none
where the time goes in v2:
time: 49.7 us; the launch traced here: 49.5 us
  Pallas kernels  48.9 us (98%)
  between operations  0.64 us (1%)
    pallas_call x1, Pallas kernels, per_device(): pl.pallas_call(kernel, out_shape=tuple((pltpu.VMEM(s.shape, s.dtype) for...  48.2 us

profile of v2, /device:TPU:1, one launch (start us, length us, event | category | flops | bytes accessed | tf_op | source)
XLA Modules:
  0.0 49.5 jit_solution(17202485396565669843)
XLA Ops:
  0.6 48.2 %update_and_apply.1 = (bf16[1,256,512]{2,1,0:T(8,128)(2,1)S(1)}, f32[1,4,512]{2,1,0:T(4,128)S(1)}, f32[1,4,512]{2,1,0:T(4,128)S(1)}) custom-call(bf16[1,256,512]{2,1,0:T(8,128)(2,1)} %keys.1, bf16[1,256,512]{2,1,0:T(8,128)(2,1)} %values.1, bf16[1,256,512]{2,1,0:T(8,128)(2,1)} %queries.1, f32[1,256]{1,0:T(1,128)} %lr.1, bf16[1,512,512]{2,1,0:T(8,128)(2,1)} %w_gate.1, ...), custom_call_target="tpu_custom_call" | custom-call | flops 1073741824 | bytes 3145728 | tf_op jit(solution)/shard_map/update_and_apply/pallas_call | solution.py:268
  48.8 0.7 %store.1 = (bf16[1,256,512]{2,1,0:T(8,128)(2,1)}, f32[1,4,512]{2,1,0:T(4,128)}, f32[1,4,512]{2,1,0:T(4,128)}) custom-call(bf16[1,256,512]{2,1,0:T(8,128)(2,1)S(1)} %get-tuple-element.6.a, f32[1,4,512]{2,1,0:T(4,128)S(1)} %get-tuple-element.7.b, f32[1,4,512]{2,1,0:T(4,128)S(1)} %get-tuple-element.8.c), custom_call_target="tpu_custom_call" | custom-call | tf_op jit(solution)/shard_map/store/pallas_call | solution.py:311

commit v3 on v2

--- a/solution.py
+++ b/solution.py
@@ -10,7 +10,9 @@
 RING = 8
 D = 512
 T = 256
-Y_ORDER = (1, 0, 2, 3, 7, 6, 4, 5)
+PARTS = 2
+PART = 64 // PARTS
+Y_ORDER = (0, 1, 2, 3, 7, 6, 4, 5)
 Z_ORDER = (0, 1, 2, 3, 4, 5, 6, 7)
 NEAR_FIRST = (1, 7, 2, 6, 3, 5, 4)
 
@@ -135,9 +137,16 @@
     mom_copy = remote(mom_v.at[other], mom_in, mom_ss.at[0], mom_rs.at[0], partner)
     mom_copy.start()
 
-    def hop(s):
-        return remote(hop_send.at[s], hop_recv.at[at1], hop_ss.at[s], hop_rs.at[at1], first(s))
-
+    def span(h):
+        return pl.ds(h * PART, PART)
+
+    def hop(s, h, slot=None):
+        slot = at1 if slot is None else slot
+        return remote(
+            hop_send.at[s, span(h)], hop_recv.at[slot, span(h)], hop_ss.at[s, h], hop_rs.at[slot, h], first(s)
+        )
+
+    sent = []
     for copy, t in zip(pairs, turns):
         g = ((at1 >> 1) + t) & 3
         rows = pl.ds(pl.multiple_of(g * 128, 128), 128)
@@ -148,13 +157,18 @@
             for half in range(2):
                 s = 2 * g + half
                 hop_send[s] = part[64 * half : 64 * half + 64].astype(BF16)
-                hop(s).start()
+                hop(s, 0).start()
+                sent.append(s)
         else:
             low = (at1 & 1) == 0
             total[...] = jnp.where(low, part[:64], part[64:])
             s = at1 + 1 - 2 * (at1 & 1)
             hop_send[s] = jnp.where(low, part[64:], part[:64]).astype(BF16)
-            hop(s).start()
+            hop(s, 0).start()
+            sent.append(s)
+    for h in range(1, PARTS):
+        for s in sent:
+            hop(s, h).start()
 
     loads[8].wait()
     order = one_hot(swapped(lax.broadcasted_iota(jnp.int32, (D, 128), 0)), D)
@@ -168,65 +182,74 @@
     momentum = jnp.concatenate([jnp.where(even, own, given), jnp.where(even, given, own)], axis=0)
     total[here, :] = total[here, :] + 0.9 * momentum
 
-    acc = total[...]
-    for k in NEAR_FIRST:
-        s = beside(at1, k)
-        remote(hop_send.at[s], hop_recv.at[s], hop_ss.at[s], hop_rs.at[s], first(s)).wait_recv()
-        acc = acc + hop_recv[s].astype(F32)
-    part_send[...] = acc.astype(BF16)
-
-    def share(s):
-        return remote(part_send, part_recv.at[at2], part_ss.at[s], part_rs.at[at2], second(s))
-
-    for sy, sz in zip(Y_ORDER, Z_ORDER):
-        s = jnp.where(even, sz, sy)
-
-        @pl.when(s != at2)
-        def _(s=s):
-            share(s).start()
-
-    for k in NEAR_FIRST:
-        s = beside(at2, k)
-        remote(part_send, part_recv.at[s], part_ss.at[s], part_rs.at[s], second(s)).wait_recv()
-        acc = acc + part_recv[s].astype(F32)
-    scale = 0.02 / jnp.sqrt(jnp.mean(acc * acc, axis=1, keepdims=True) + 1e-05)
-
-    def block(s):
-        return weights.at[mine, pl.ds(pl.multiple_of(s * 64, 64), 64)]
-
-    block(at1)[...] = (w_rows - acc * scale).astype(BF16)
-
-    def spread(s):
-        return remote(block(at1), block(at1), far_ss.at[s], far_rs.at[at1], first(s))
-
-    def forward(s):
-        return remote(block(s), block(s), fwd_ss.at[s], fwd_rs.at[s], partner)
-
-    for sy, sz in zip(Y_ORDER, Z_ORDER):
-        s = jnp.where(even, sy, sz)
-
-        @pl.when(s != at1)
-        def _(s=s):
-            spread(s).start()
-
-    forward(at1).start()
-    total[...] = acc
+    def share(s, h, slot=None):
+        slot = at2 if slot is None else slot
+        return remote(
+            part_send.at[span(h)], part_recv.at[slot, span(h)], part_ss.at[s, h], part_rs.at[slot, h], second(s)
+        )
+
+    sums = []
+    for h in range(PARTS):
+        acc = total[span(h), :]
+        for k in NEAR_FIRST:
+            s = beside(at1, k)
+            hop(s, h, s).wait_recv()
+            acc = acc + hop_recv[s, span(h), :].astype(F32)
+        sums.append(acc)
+        part_send[span(h), :] = acc.astype(BF16)
+        for sy, sz in zip(Y_ORDER, Z_ORDER):
+            s = jnp.where(even, sz, sy)
+
+            @pl.when(s != at2)
+            def _(s=s):
+                share(s, h).start()
+
+    def block(matrix, s, h):
+        return weights.at[matrix, pl.ds(pl.multiple_of(s * 64 + h * PART, PART), PART)]
+
+    def spread(s, h, slot=None):
+        slot = at1 if slot is None else slot
+        rows = block(mine, slot, h)
+        return remote(rows, rows, far_ss.at[s, h], far_rs.at[slot, h], first(s))
+
+    def forward(s, h):
+        return remote(block(mine, s, h), block(mine, s, h), fwd_ss.at[s, h], fwd_rs.at[s, h], partner)
+
+    for h in range(PARTS):
+        acc = sums[h]
+        for k in NEAR_FIRST:
+            s = beside(at2, k)
+            share(s, h, s).wait_recv()
+            acc = acc + part_recv[s, span(h), :].astype(F32)
+        total[span(h), :] = acc
+        scale = 0.02 / jnp.sqrt(jnp.mean(acc * acc, axis=1, keepdims=True) + 1e-05)
+        block(mine, at1, h)[...] = (w_rows[h * PART : h * PART + PART] - acc * scale).astype(BF16)
+        for sy, sz in zip(Y_ORDER, Z_ORDER):
+            s = jnp.where(even, sy, sz)
+
+            @pl.when(s != at1)
+            def _(s=s):
+                spread(s, h).start()
+
+        forward(at1, h).start()
     fresh = total[here, :]
     keep = jnp.where(even, fresh[:4], fresh[4:])
     mom_send[...] = jnp.where(even, fresh[4:], fresh[:4])
     mom_back = remote(mom_send, mom_recv, mom_ss.at[1], mom_rs.at[1], partner)
     mom_back.start()
-    for k in NEAR_FIRST:
-        s = beside(at1, k)
-        remote(block(s), block(s), far_ss.at[s], far_rs.at[s], first(s)).wait_recv()
-        forward(s).start()
+    for h in range(PARTS):
+        for k in NEAR_FIRST:
+            s = beside(at1, k)
+            spread(s, h, s).wait_recv()
+            forward(s, h).start()
     mom_back.wait_recv()
     back = mom_recv[...]
     out_gate[0] = jnp.where(even, keep, back)
     out_up[0] = jnp.where(even, back, keep)
-    for s in range(RING):
-        theirs_s = weights.at[other, pl.ds(64 * s, 64)]
-        remote(theirs_s, theirs_s, fwd_ss.at[s], fwd_rs.at[s], partner).wait_recv()
+    for h in range(PARTS):
+        for s in range(RING):
+            rows = block(other, s, h)
+            remote(rows, rows, fwd_ss.at[s, h], fwd_rs.at[s, h], partner).wait_recv()
 
     for h in range(2):
         cols = pl.ds(h * (D // 2), D // 2)
@@ -235,12 +258,13 @@
         grads[0, :, cols] = (gate * jax.nn.sigmoid(gate) * up).astype(BF16)
     out[0] = dot(grads[0], down_v[...]).astype(BF16)
 
-    for k in range(1, RING):
-        hop(beside(at1, k)).wait_send()
-        share(beside(at2, k)).wait_send()
-        spread(beside(at1, k)).wait_send()
-    for s in range(RING):
-        forward(s).wait_send()
+    for h in range(PARTS):
+        for k in range(1, RING):
+            hop(beside(at1, k), h).wait_send()
+            share(beside(at2, k), h).wait_send()
+            spread(beside(at1, k), h).wait_send()
+        for s in range(RING):
+            forward(s, h).wait_send()
     for copy in pairs + [mom_copy, mom_back]:
         copy.wait_send()
 
@@ -294,10 +318,10 @@
             pltpu.VMEM((T, D), BF16),
             dma((9,)),
             dma((4,)), dma((4,)),
-            dma((RING,)), dma((RING,)),
-            dma((RING,)), dma((RING,)),
-            dma((RING,)), dma((RING,)),
-            dma((RING,)), dma((RING,)),
+            dma((RING, PARTS)), dma((RING, PARTS)),
+            dma((RING, PARTS)), dma((RING, PARTS)),
+            dma((RING, PARTS)), dma((RING, PARTS)),
+            dma((RING, PARTS)), dma((RING, PARTS)),
             dma((2,)), dma((2,)),
         ],
         compiler_params=pltpu.CompilerParams(

time: 49.7 us -> 46.8 us (0.942)
  Pallas kernels: 48.9 us -> 46 us
    pallas_call x1, Pallas kernels: 48.2 us -> 45.3 us  [per_device(): pl.pallas_call(kernel, out_shape=tuple((pltpu.VMEM(s.shape, s.dtype) for...]
where the time goes in v3:
time: 46.8 us; the launch traced here: 46.6 us
  Pallas kernels  46 us (98%)
  between operations  0.64 us (1%)
    pallas_call x1, Pallas kernels, per_device(): pl.pallas_call(kernel, out_shape=tuple((pltpu.VMEM(s.shape, s.dtype) for...  45.3 us

profile of v3, /device:TPU:1, one launch (start us, length us, event | category | flops | bytes accessed | tf_op | source)
XLA Modules:
  0.0 46.6 jit_solution(15595792288642605490)
XLA Ops:
  0.6 45.3 %update_and_apply.1 = (bf16[1,256,512]{2,1,0:T(8,128)(2,1)S(1)}, f32[1,4,512]{2,1,0:T(4,128)S(1)}, f32[1,4,512]{2,1,0:T(4,128)S(1)}) custom-call(bf16[1,256,512]{2,1,0:T(8,128)(2,1)} %keys.1, bf16[1,256,512]{2,1,0:T(8,128)(2,1)} %values.1, bf16[1,256,512]{2,1,0:T(8,128)(2,1)} %queries.1, f32[1,256]{1,0:T(1,128)} %lr.1, bf16[1,512,512]{2,1,0:T(8,128)(2,1)} %w_gate.1, ...), custom_call_target="tpu_custom_call" | custom-call | flops 1073741824 | bytes 3145728 | tf_op jit(solution)/shard_map/update_and_apply/pallas_call | solution.py:292
  45.9 0.7 %store.1 = (bf16[1,256,512]{2,1,0:T(8,128)(2,1)}, f32[1,4,512]{2,1,0:T(4,128)}, f32[1,4,512]{2,1,0:T(4,128)}) custom-call(bf16[1,256,512]{2,1,0:T(8,128)(2,1)S(1)} %get-tuple-element.6.a, f32[1,4,512]{2,1,0:T(4,128)S(1)} %get-tuple-element.7.b, f32[1,4,512]{2,1,0:T(4,128)S(1)} %get-tuple-element.8.c), custom_call_target="tpu_custom_call" | custom-call | tf_op jit(solution)/shard_map/store/pallas_call | solution.py:335

commit v4 on v3

--- a/solution.py
+++ b/solution.py
@@ -120,8 +120,6 @@
         grads[0, :, cols] = (zs * up * (1.0 + gate * (1.0 - sig))).astype(BF16)
         grads[1, :, cols] = (zs * gate).astype(BF16)
 
-    pl.semaphore_wait(barrier, 2 * RING - 1)
-
     turns = (2, 1, 3, 0)
     theirs = jnp.where(even, z, y) >> 1
     pairs = []
@@ -129,9 +127,10 @@
         g = (theirs + t) & 3
         rows = pl.ds(pl.multiple_of(g * 128, 128), 128)
         pair_send[rows, :] = dot(keys_t[other, rows, :], grads[other]).astype(BF16)
-        copy = remote(pair_send.at[rows], pair_recv.at[rows], pair_ss.at[t], pair_rs.at[t], partner)
+        pairs.append(remote(pair_send.at[rows], pair_recv.at[rows], pair_ss.at[t], pair_rs.at[t], partner))
+    pl.semaphore_wait(barrier, 2 * RING - 1)
+    for copy in pairs:
         copy.start()
-        pairs.append(copy)
     loads[6].wait()
     loads[7].wait()
     mom_copy = remote(mom_v.at[other], mom_in, mom_ss.at[0], mom_rs.at[0], partner)
@@ -212,8 +211,9 @@
         rows = block(mine, slot, h)
         return remote(rows, rows, far_ss.at[s, h], far_rs.at[slot, h], first(s))
 
-    def forward(s, h):
-        return remote(block(mine, s, h), block(mine, s, h), fwd_ss.at[s, h], fwd_rs.at[s, h], partner)
+    def forward(s, matrix=None):
+        rows = weights.at[mine if matrix is None else matrix, pl.ds(pl.multiple_of(s * 64, 64), 64)]
+        return remote(rows, rows, fwd_ss.at[s, 0], fwd_rs.at[s, 0], partner)
 
     for h in range(PARTS):
         acc = sums[h]
@@ -231,25 +231,33 @@
             def _(s=s):
                 spread(s, h).start()
 
-        forward(at1, h).start()
+    forward(at1).start()
     fresh = total[here, :]
     keep = jnp.where(even, fresh[:4], fresh[4:])
     mom_send[...] = jnp.where(even, fresh[4:], fresh[:4])
     mom_back = remote(mom_send, mom_recv, mom_ss.at[1], mom_rs.at[1], partner)
     mom_back.start()
     for h in range(PARTS):
+        for k in range(1, RING):
+            hop(beside(at1, k), h).wait_send()
+            share(beside(at2, k), h).wait_send()
+    for copy in pairs + [mom_copy]:
+        copy.wait_send()
+    for h in range(PARTS):
         for k in NEAR_FIRST:
             s = beside(at1, k)
             spread(s, h, s).wait_recv()
-            forward(s, h).start()
+            if h == PARTS - 1:
+                forward(s).start()
+    for h in range(PARTS):
+        for k in range(1, RING):
+            spread(beside(at1, k), h).wait_send()
     mom_back.wait_recv()
     back = mom_recv[...]
     out_gate[0] = jnp.where(even, keep, back)
     out_up[0] = jnp.where(even, back, keep)
-    for h in range(PARTS):
-        for s in range(RING):
-            rows = block(other, s, h)
-            remote(rows, rows, fwd_ss.at[s, h], fwd_rs.at[s, h], partner).wait_recv()
+    for s in range(RING):
+        forward(s, other).wait_recv()
 
     for h in range(2):
         cols = pl.ds(h * (D // 2), D // 2)
@@ -258,15 +266,9 @@
         grads[0, :, cols] = (gate * jax.nn.sigmoid(gate) * up).astype(BF16)
     out[0] = dot(grads[0], down_v[...]).astype(BF16)
 
-    for h in range(PARTS):
-        for k in range(1, RING):
-            hop(beside(at1, k), h).wait_send()
-            share(beside(at2, k), h).wait_send()
-            spread(beside(at1, k), h).wait_send()
-        for s in range(RING):
-            forward(s, h).wait_send()
-    for copy in pairs + [mom_copy, mom_back]:
-        copy.wait_send()
+    for s in range(RING):
+        forward(s).wait_send()
+    mom_back.wait_send()
 
 
 def store_kernel(a, b, c, a_out, b_out, c_out, sem):

time: 46.8 us -> 46.1 us (0.985)
  Pallas kernels: 46 us -> 45.3 us
    pallas_call x1, Pallas kernels: 45.3 us -> 44.5 us  [per_device(): pl.pallas_call(kernel, out_shape=tuple((pltpu.VMEM(s.shape, s.dtype) for...]
where the time goes in v4:
time: 46.1 us; the launch traced here: 45.9 us
  Pallas kernels  45.3 us (98%)
  between operations  0.64 us (1%)
    pallas_call x1, Pallas kernels, per_device(): pl.pallas_call(kernel, out_shape=tuple((pltpu.VMEM(s.shape, s.dtype) for...  44.5 us

profile of v4, /device:TPU:1, one launch (start us, length us, event | category | flops | bytes accessed | tf_op | source)
XLA Modules:
  0.0 45.9 jit_solution(4630709187784784419)
XLA Ops:
  0.6 44.5 %update_and_apply.1 = (bf16[1,256,512]{2,1,0:T(8,128)(2,1)S(1)}, f32[1,4,512]{2,1,0:T(4,128)S(1)}, f32[1,4,512]{2,1,0:T(4,128)S(1)}) custom-call(bf16[1,256,512]{2,1,0:T(8,128)(2,1)} %keys.1, bf16[1,256,512]{2,1,0:T(8,128)(2,1)} %values.1, bf16[1,256,512]{2,1,0:T(8,128)(2,1)} %queries.1, f32[1,256]{1,0:T(1,128)} %lr.1, bf16[1,512,512]{2,1,0:T(8,128)(2,1)} %w_gate.1, ...), custom_call_target="tpu_custom_call" | custom-call | flops 1073741824 | bytes 3145728 | tf_op jit(solution)/shard_map/update_and_apply/pallas_call | solution.py:294
  45.2 0.7 %store.1 = (bf16[1,256,512]{2,1,0:T(8,128)(2,1)}, f32[1,4,512]{2,1,0:T(4,128)}, f32[1,4,512]{2,1,0:T(4,128)}) custom-call(bf16[1,256,512]{2,1,0:T(8,128)(2,1)S(1)} %get-tuple-element.6.a, f32[1,4,512]{2,1,0:T(4,128)S(1)} %get-tuple-element.7.b, f32[1,4,512]{2,1,0:T(4,128)S(1)} %get-tuple-element.8.c), custom_call_target="tpu_custom_call" | custom-call | tf_op jit(solution)/shard_map/store/pallas_call | solution.py:337
